TPU v7x, 32 devices: a whole 2x2x4 slice. The times are simulated.
32 devices in a mesh: dp: 4 (over x, core), seq: 8 (over z, y).
Axes of the slice: x: 2, y: 2, z: 4, core: 2. Of those that a mesh axis runs over, the one named last changes fastest.
Arguments:
- inputs: bfloat16 [8, 4096, 512], P('dp', 'seq'), may hold values from -6 to 6
- segment_ids: int32 [8, 4096], P('dp', 'seq'), may hold values from 0 to 4095, as said below
- real_block: int32 [8, 128], P('dp', 'seq'), may hold values from 0 to 1, as said below
- gain_attn: bfloat16 [512], replicated, may hold values from 0.25 to 1.75
- w_query: bfloat16 [512, 512], replicated, may hold values from -0.25 to 0.25
- w_key: bfloat16 [512, 512], replicated, may hold values from -0.25 to 0.25
- w_value: bfloat16 [512, 512], replicated, may hold values from -0.25 to 0.25
- w_output: bfloat16 [512, 512], replicated, may hold values from -2 to 2
- w_sort: bfloat16 [512, 512], replicated, may hold values from -0.25 to 0.25
- gain_ffn: bfloat16 [512], replicated, may hold values from 0.25 to 1.75
- w_in: bfloat16 [512, 2048], replicated, may hold values from -0.25 to 0.25
- w_out: bfloat16 [2048, 512], replicated, may hold values from -0.125 to 0.125
- cotangent: bfloat16 [8, 4096, 512], P('dp', 'seq'), may hold values from -6 to 6
Outputs:
- output: bfloat16 [8, 4096, 512], P('dp', 'seq')
- input_grad: bfloat16 [8, 4096, 512], P('dp', 'seq')
- penalty: float32 [], replicated
- grad_gain_attn: float32 [512], replicated
- grad_query: float32 [512, 512], replicated
- grad_key: float32 [512, 512], replicated
- grad_value: float32 [512, 512], replicated
- grad_output: float32 [512, 512], replicated
- grad_sort: float32 [512, 512], replicated
- slope_feedforward_scaler: float32 [512], replicated
- grad_in: float32 [512, 2048], replicated
- grad_out: float32 [2048, 512], replicated
Inputs may be any that keep to these rules, and one draw needn't show every extreme that they name: `segment_ids`: Non-decreasing along each sequence; the ids of the pack that begins at position p * 256 lie in p * 256 to p * 256 + 255, so ids of different packs differ; the last position of every sequence holds the top id of its pack. `real_block`: the last block of every sequence is 1.
All inputs are finite; a program needn't handle non-finite values.
Results may differ from a plain program's by a relative error of at most 0.035.
Values may be sent and summed in bfloat16 or wider, within the bound.
No kernel may reach another device: no remote copies, remote signals or barrier semaphores. Data moves between devices by JAX's collectives and lax.ppermute only.
A program may use at most 384 MiB of HBM per device.

v0:
```python
import math

import jax
import jax.numpy as jnp
from jax import lax
from jax.sharding import PartitionSpec as P

HEADS = 8
BLOCK = 32
ITERS = 8


EPS = 1e-06
NEG = -1000000000.0
SORT_GAIN = 2.5


def normalize(payload_vector_entries, gain_vec):
    inv_rms = lax.rsqrt(
        jnp.mean(payload_vector_entries * payload_vector_entries, axis=-1, keepdims=True) + EPS
    )
    unit_vals = payload_vector_entries * inv_rms
    return (unit_vals * gain_vec, unit_vals, inv_rms)


def norm_back(upstream, unit_vals, inv_rms, gain_vec):
    d_unit = upstream * gain_vec
    d_values = inv_rms * (d_unit - unit_vals * jnp.mean(d_unit * unit_vals, axis=-1, keepdims=True))
    return (d_values, jnp.sum(upstream * unit_vals, axis=(0, 1)))


def doubly_stochastic_normalizer(permutation_raw_scores, retained_target_slots):
    keep_mask = retained_target_slots[:, None, :]
    logarithmic_coupling_matrix = jnp.where(keep_mask, permutation_raw_scores, NEG)
    for sweep_index in range(ITERS):
        logarithmic_coupling_matrix = logarithmic_coupling_matrix - jax.nn.logsumexp(
            logarithmic_coupling_matrix, axis=2, keepdims=True
        )
        logarithmic_coupling_matrix = logarithmic_coupling_matrix - jnp.where(
            keep_mask, jax.nn.logsumexp(logarithmic_coupling_matrix, axis=1, keepdims=True), 0.0
        )
    return logarithmic_coupling_matrix


def product(left_mat, right_mat):
    return lax.dot_general(
        left_mat,
        right_mat,
        (((left_mat.ndim - 1,), (0,)), ((), ())),
        preferred_element_type=jnp.float32,
    )


def product_back(left_mat, right_mat):
    return lax.dot_general(
        left_mat,
        right_mat,
        (((left_mat.ndim - 1,), (1,)), ((), ())),
        preferred_element_type=jnp.float32,
    )


def weight_grad(left_mat, right_mat):
    flat_left = left_mat.reshape(-1, left_mat.shape[-1])
    flat_right = right_mat.reshape(-1, right_mat.shape[-1])
    return lax.dot_general(
        flat_left, flat_right, (((0,), (0,)), ((), ())), preferred_element_type=jnp.float32
    )


def attend_scores(queries, key_all, segments, att_scale):
    scores = (
        jnp.einsum("snthd,snkhd->snhtk", queries, key_all, preferred_element_type=jnp.float32)
        * att_scale
    )
    same_seg = segments[:, :, :, None] == segments[:, :, None, :]
    allowed = jnp.concatenate([same_seg, jnp.ones_like(same_seg)], axis=-1)[:, :, None]
    return jnp.where(allowed, scores, NEG)


def body(
    inputs,
    segment_ids,
    real_block,
    gain_attn,
    w_query,
    w_key,
    w_value,
    w_output,
    w_sort,
    gain_ffn,
    w_in,
    w_out,
    cotangent,
):
    seq_count, span_len, model_width = inputs.shape
    local_blocks = span_len // BLOCK
    head_dim = model_width // HEADS
    flat_width = BLOCK * model_width
    att_scale = 1.0 / math.sqrt(head_dim)
    sort_scale = SORT_GAIN * BLOCK / math.sqrt(model_width)
    first_block = lax.axis_index("seq") * local_blocks
    count_mine = jnp.sum(real_block).astype(jnp.float32)
    block_grand_total = lax.psum(count_mine, ("dp", "seq"))
    inputs_f = inputs.astype(jnp.float32)
    gain_one = gain_attn.astype(jnp.float32)
    gain_two = gain_ffn.astype(jnp.float32)
    normed, leading_identity_scalar, scale_one = normalize(inputs_f, gain_one)
    hidden = normed.astype(jnp.bfloat16)
    blocks = hidden.reshape(seq_count, local_blocks, BLOCK, model_width)
    blocks_flat = blocks.reshape(seq_count, local_blocks, flat_width)
    summary = jnp.mean(blocks, axis=2, dtype=jnp.float32).astype(jnp.bfloat16)
    summary_all, real_all = (
        lax.all_gather(summary, "seq", axis=1, tiled=True),
        lax.all_gather(real_block.astype(jnp.bfloat16), "seq", axis=1, tiled=True),
    )
    retained_target_slots = real_all == 1
    sort_proj = product(summary_all, w_sort).astype(jnp.bfloat16)
    permutation_raw_scores = sort_scale * jnp.einsum(
        "sid,sjd->sij", sort_proj, summary_all, preferred_element_type=jnp.float32
    )

    def plan_of(payload_vector_entries):
        return doubly_stochastic_normalizer(payload_vector_entries, retained_target_slots)

    logarithmic_coupling_matrix, plan_back = jax.vjp(plan_of, permutation_raw_scores)
    prob_full = jnp.exp(logarithmic_coupling_matrix)
    plan_rows = lax.dynamic_slice_in_dim(logarithmic_coupling_matrix, first_block, local_blocks, 1)
    entropy_mine = jnp.sum(
        jnp.where((real_block == 1)[:, :, None], jnp.exp(plan_rows) * plan_rows, 0.0)
    )
    prob_low = prob_full.astype(jnp.bfloat16)
    prob_rows = lax.dynamic_slice_in_dim(prob_low, first_block, local_blocks, 1)
    shard_piece = lax.all_gather(blocks, "seq", axis=1, tiled=True)
    flat_piece = shard_piece.reshape(seq_count, shard_piece.shape[1], flat_width)
    prob_part = prob_rows
    mixed_sum = jnp.einsum(
        "sim,smf->sif", prob_part, flat_piece, preferred_element_type=jnp.float32
    )
    mixed = mixed_sum.astype(jnp.bfloat16).reshape(seq_count, local_blocks, BLOCK, model_width)
    shape_heads = (seq_count, local_blocks, BLOCK, HEADS, head_dim)
    queries = product(hidden, w_query).astype(jnp.bfloat16).reshape(shape_heads)
    key_local = product(hidden, w_key).astype(jnp.bfloat16).reshape(shape_heads)
    value_local = product(hidden, w_value).astype(jnp.bfloat16).reshape(shape_heads)
    key_sorted = product(mixed, w_key).astype(jnp.bfloat16).reshape(shape_heads)
    value_sorted = product(mixed, w_value).astype(jnp.bfloat16).reshape(shape_heads)
    key_all = jnp.concatenate([key_local, key_sorted], axis=2)
    value_all = jnp.concatenate([value_local, value_sorted], axis=2)
    segments = segment_ids.reshape(seq_count, local_blocks, BLOCK)
    scores = attend_scores(queries, key_all, segments, att_scale)
    peak_score = jnp.max(scores, axis=-1, keepdims=True)
    exponent = jnp.exp(scores - peak_score)
    denominator = jnp.sum(exponent, axis=-1, keepdims=True)
    log_total = peak_score + jnp.log(denominator)
    weights_low = (exponent / denominator).astype(jnp.bfloat16)
    attended = jnp.einsum(
        "snhtk,snkhd->snthd", weights_low, value_all, preferred_element_type=jnp.float32
    )
    attended = attended.astype(jnp.bfloat16).reshape(seq_count, span_len, model_width)
    residual = inputs_f + product(attended, w_output)
    normed_two, unit_two, scale_two = normalize(residual, gain_two)
    hidden_two = normed_two.astype(jnp.bfloat16)
    pre_act = product(hidden_two, w_in)
    activation, gelu_back = jax.vjp(jax.nn.gelu, pre_act)
    activation_low = activation.astype(jnp.bfloat16)
    output = (residual + product(activation_low, w_out)).astype(jnp.bfloat16)
    grad_out = weight_grad(activation_low, cotangent)
    (d_pre,) = gelu_back(product_back(cotangent, w_out))
    d_pre_low = d_pre.astype(jnp.bfloat16)
    grad_in = weight_grad(hidden_two, d_pre_low)
    d_resid, grad_gain_two = norm_back(product_back(d_pre_low, w_in), unit_two, scale_two, gain_two)
    d_resid = d_resid + cotangent.astype(jnp.float32)
    d_branch = d_resid.astype(jnp.bfloat16)
    grad_output = weight_grad(attended, d_branch)
    d_att = product_back(d_branch, w_output).astype(jnp.bfloat16).reshape(shape_heads)
    weights_full = jnp.exp(attend_scores(queries, key_all, segments, att_scale) - log_total)
    d_weights = jnp.einsum(
        "snthd,snkhd->snhtk", d_att, value_all, preferred_element_type=jnp.float32
    )
    d_scores = weights_full * (
        d_weights - jnp.sum(weights_full * d_weights, axis=-1, keepdims=True)
    )
    d_scores = d_scores.astype(jnp.bfloat16)
    d_query = (
        att_scale
        * jnp.einsum("snhtk,snkhd->snthd", d_scores, key_all, preferred_element_type=jnp.float32)
    ).astype(jnp.bfloat16)
    cotangent_lookup_vectors = (
        att_scale
        * jnp.einsum("snhtk,snthd->snkhd", d_scores, queries, preferred_element_type=jnp.float32)
    ).astype(jnp.bfloat16)
    d_vals = jnp.einsum(
        "snhtk,snthd->snkhd", weights_low, d_att, preferred_element_type=jnp.float32
    ).astype(jnp.bfloat16)
    d_query = d_query.reshape(seq_count, span_len, model_width)
    d_key_local = cotangent_lookup_vectors[:, :, :BLOCK].reshape(seq_count, span_len, model_width)
    d_key_sorted = cotangent_lookup_vectors[:, :, BLOCK:].reshape(
        seq_count, local_blocks, BLOCK, model_width
    )
    d_value_local = d_vals[:, :, :BLOCK].reshape(seq_count, span_len, model_width)
    d_value_sorted = d_vals[:, :, BLOCK:].reshape(seq_count, local_blocks, BLOCK, model_width)
    grad_query = weight_grad(hidden, d_query)
    grad_key = weight_grad(hidden, d_key_local) + weight_grad(mixed, d_key_sorted)
    grad_value = weight_grad(hidden, d_value_local) + weight_grad(mixed, d_value_sorted)
    d_hidden = (
        product_back(d_query, w_query)
        + product_back(d_key_local, w_key)
        + product_back(d_value_local, w_value)
    )
    mixed_gradient = (
        product_back(d_key_sorted, w_key) + product_back(d_value_sorted, w_value)
    ).astype(jnp.bfloat16)
    prob_cols = lax.dynamic_slice_in_dim(prob_low, first_block, local_blocks, 2)
    shard_piece = lax.all_gather(mixed_gradient, "seq", axis=1, tiled=True)
    flat_piece = shard_piece.reshape(seq_count, shard_piece.shape[1], flat_width)
    prob_part = prob_cols
    block_sum = jnp.einsum(
        "smj,smf->sjf", prob_part, flat_piece, preferred_element_type=jnp.float32
    )
    found_grads = jnp.einsum(
        "smf,sjf->smj", flat_piece, blocks_flat, preferred_element_type=jnp.float32
    )
    d_prob = lax.all_gather(found_grads.astype(jnp.bfloat16), "seq", axis=2, tiled=True).astype(
        found_grads.dtype
    )
    entropy_grad = jnp.where(
        retained_target_slots[:, :, None], prob_full * logarithmic_coupling_matrix + prob_full, 0.0
    )
    d_plan = prob_full * d_prob - entropy_grad / block_grand_total
    (d_logits,) = plan_back(d_plan)
    d_logits = d_logits.astype(jnp.bfloat16)
    rows_grad = lax.dynamic_slice_in_dim(d_logits, first_block, local_blocks, 1)
    cols_grad = lax.dynamic_slice_in_dim(d_logits, first_block, local_blocks, 2)
    d_proj = (
        sort_scale
        * jnp.einsum("sij,sjd->sid", rows_grad, summary_all, preferred_element_type=jnp.float32)
    ).astype(jnp.bfloat16)
    grad_sort = weight_grad(summary, d_proj)
    d_summary = sort_scale * jnp.einsum(
        "sij,sid->sjd", cols_grad, sort_proj, preferred_element_type=jnp.float32
    ) + product_back(d_proj, w_sort)
    d_hidden = (
        d_hidden.reshape(seq_count, local_blocks, BLOCK, model_width)
        + block_sum.reshape(seq_count, local_blocks, BLOCK, model_width)
        + d_summary[:, :, None, :] / BLOCK
    )
    d_input, grad_gain_one = norm_back(
        d_hidden.reshape(seq_count, span_len, model_width),
        leading_identity_scalar,
        scale_one,
        gain_one,
    )
    input_grad = (d_input + d_resid).astype(jnp.bfloat16)
    totals = lax.psum(
        (
            grad_gain_one,
            grad_query,
            grad_key,
            grad_value,
            grad_output,
            grad_sort,
            grad_gain_two,
            grad_in,
            grad_out,
            entropy_mine,
        ),
        ("dp", "seq"),
    )
    penalty = -totals[9] / block_grand_total
    return (output, input_grad, penalty) + tuple(totals[:9])


def solution(mesh):
    placed = (
        P("dp", "seq", None),
        P("dp", "seq"),
        P("dp", "seq"),
        P(),
        P(),
        P(),
        P(),
        P(),
        P(),
        P(),
        P(),
        P(),
        P("dp", "seq", None),
    )
    return jax.shard_map(
        body,
        mesh=mesh,
        in_specs=placed,
        out_specs=(
            P("dp", "seq", None),
            P("dp", "seq", None),
            P(),
            P(),
            P(),
            P(),
            P(),
            P(),
            P(),
            P(),
            P(),
            P(),
        ),
        check_vma=False,
    )
```

profile of v0, /device:TPU:0, one launch (start us, length us, event | category | flops | bytes accessed | tf_op | source)
XLA Modules:
  0.0 735.7 jit_solution(18033573663700563306)
XLA Ops:
  13.7 22.3 %all-gather = bf16[8,16,2]{1,2,0:T(2,128)(2,1)S(1)} all-gather(bf16[1,16,2]{1,2,0:T(2,128)(2,1)S(1)} %get-tuple-element.43), channel_id=1, replica_groups=mesh['dp'=4,'seq'=8] {'seq'}, dimensions={0}, use_global_device_ids=true | all-gather | bytes 576 | tf_op jit(solution)/shard_map/all_gather | solution.py:115
  36.1 3.0 convolution_convert_fusion.3
  39.2 3.9 reshape.520
  45.8 3.9 reshape.519
  52.4 3.9 reshape.514
  57.3 32.2 %all_gather.16 = bf16[2,128,512]{2,1,0:T(8,128)(2,1)S(1)} all-gather(bf16[2,16,512]{2,1,0:T(8,128)(2,1)S(1)} %multiply_convert_fusion.7), channel_id=1, replica_groups=mesh['dp'=4,'seq'=8] {'seq'}, dimensions={1}, use_global_device_ids=true | all-gather | bytes 294912 | tf_op jit(solution)/shard_map/all_gather | solution.py:114
  118.0 24.7 %all-gather.4.cloned.1.call-done = bf16[2,128,32,512]{3,2,1,0:T(8,128)(2,1)} async-done(((bf16[2,16,32,512]{3,2,1,0:T(8,128)(2,1)}), bf16[2,128,32,512]{3,2,1,0:T(8,128)(2,1)}) %all-gather.4.cloned.1.call-update) | async-done | bytes 8388624 | tf_op jit(solution)/shard_map/all_gather | solution.py:134
  142.7 13.6 %reshape.516 = bf16[2,128,16384]{2,1,0:T(8,128)(2,1)} reshape(bf16[2,128,32,512]{3,2,1,0:T(8,128)(2,1)} %all-gather.4.cloned.1.call-done) | data formatting | bytes 16777216 | tf_op jit(solution)/shard_map/reshape | solution.py:135
  156.3 4.7 convolution_convert_fusion
  164.0 3.9 reshape.518
  167.9 3.0 convolution_convert_fusion.2
  171.0 3.9 reshape.521
  174.9 3.5 copy_dynamic-update-slice_fusion
  178.4 4.7 fusion.13
  187.7 3.0 convert_bitcast_fusion.1
  193.0 4.2 reshape.522
  202.1 7.4 %fusion.6 = bf16[2,512,2048]{2,1,0:T(8,128)(2,1)S(1)} fusion(f32[2,512,2048]{2,1,0:T(8,128)S(1)} %fusion.30, bf16[2,512,512]{2,1,0:T(8,128)(2,1)S(1)} %copy-done.33, bf16[2048,512]{1,0:T(8,128)(2,1)S(1)} %copy-done.123), kind=kOutput, calls=%fused_computation.9 | convolution fusion | flops 2189426688 | bytes 15728640 | tf_op jit(solution)/shard_map/dot_general | solution.py:55
  209.5 3.2 multiply_reduce_fusion.1
  216.8 2.8 reshape.523
  219.6 8.1 %convert_bitcast_fusion = bf16[2,16,64,8,64]{4,2,3,1,0:T(8,128)(2,1)} fusion(bf16[2,16,32,8,64]{4,3,2,1,0:T(8,128)(2,1)S(1)} %reshape.523, f32[2,16,8,32,64]{4,3,2,1,0:T(8,128)} %copy-done.2, f32[2,16,8,32]{3,2,1,0:T(8,128)} %copy-done.60, f32[2,16,8,32]{3,2,1,0:T(8,128)} %copy-done.44, pred[2,16,32,64]{3,2,1,0:T(8,128)(4,1)} %concatenate.11), kind=kOutput, calls=%fused_computation.13 | convolution fusion | flops 70778880 | bytes 5373952 | tf_op jit(solution)/shard_map/snhtk,snthd->snkhd/dot_general | solution.py:192
  227.7 3.2 multiply_reduce_fusion
  230.9 2.9 multiply_convert_fusion.3
  235.5 3.2 fusion.120
  243.9 3.9 copy.77
  247.8 4.0 reshape.527
  254.1 2.9 add_convert_fusion
  257.7 42.5 %psum.77 = f32[]{:T(128)} all-reduce(f32[]{:T(128)S(6)} %convert_element_type.152), channel_id=1, replica_groups=mesh['dp'=4,'seq'=8] {'dp','seq'}, use_global_device_ids=true, to_apply=%region_40.41 | all-reduce | flops 1 | bytes 8 | tf_op jit(solution)/shard_map/psum | solution.py:104
  306.9 4.3 reshape_reshape.31
  313.2 4.0 fusion.38
  323.5 4.1 reshape_reshape.30
  327.5 4.0 reshape_reshape.27
  344.6 4.6 convolution_bitcast_fusion.1
  349.2 4.7 convolution_bitcast_fusion
  353.9 28.0 %all-gather.6.cloned.1.call-done = bf16[2,128,32,512]{3,2,1,0:T(8,128)(2,1)} async-done(((bf16[2,16,32,512]{3,2,1,0:T(8,128)(2,1)}), bf16[2,128,32,512]{3,2,1,0:T(8,128)(2,1)}) %all-gather.6.cloned.1.call-update) | async-done | bytes 8388624 | tf_op jit(solution)/shard_map/all_gather | solution.py:214
  381.9 13.5 %reshape.529 = bf16[2,128,16384]{2,1,0:T(8,128)(2,1)} reshape(bf16[2,128,32,512]{3,2,1,0:T(8,128)(2,1)} %all-gather.6.cloned.1.call-done) | data formatting | bytes 16777216 | tf_op jit(solution)/shard_map/reshape | solution.py:215
  395.4 5.9 convolution_convert_fusion.8
  401.3 32.4 %all_gather.19 = bf16[2,128,128]{1,0,2:T(2,128)(2,1)} all-gather(bf16[2,128,16]{1,0,2:T(2,128)(2,1)S(1)} %copy.80), channel_id=1, replica_groups=mesh['dp'=4,'seq'=8] {'seq'}, dimensions={2}, use_global_device_ids=true | all-gather | bytes 73728 | tf_op jit(solution)/shard_map/all_gather | solution.py:223
  468.7 4.4 reshape.526
  473.1 4.1 reshape.525
  477.1 4.1 reshape.524
  481.2 3.6 fusion.53
  484.8 3.2 fusion.56
  488.1 7.4 %add_convert_fusion.1 = bf16[2,512,512]{2,1,0:T(8,128)(2,1)} fusion(f32[2,512,512]{2,1,0:T(8,128)S(1)} %copy-done.5, bf16[2048,512]{1,0:T(8,128)(2,1)S(1)} %copy-done.124, f32[2,512,2048]{2,1,0:T(8,128)} %copy-done.22), kind=kOutput, calls=%fused_computation.57 | convolution fusion | flops 2167406592 | bytes 13631488 | tf_op jit(solution)/shard_map/dot_general | solution.py:46
  498.2 2.9 reshape.530
  502.8 6.5 fusion.20
  509.2 38.5 %all-reduce.1 = (f32[]{:T(128)}, f32[512]{0:T(512)}, f32[512]{0:T(512)}) all-reduce(f32[]{:T(128)} %fusion.98, f32[512]{0:T(512)S(1)} %get-tuple-element.14, f32[512]{0:T(512)S(1)} %copy-done.119), channel_id=1, replica_groups=mesh['dp'=4,'seq'=8] {'dp','seq'}, use_global_device_ids=true, to_apply=%region_59.60 | all-reduce | flops 1025 | bytes 8200 | tf_op jit(solution)/shard_map/psum | solution.py:254
  549.1 3.9 fusion.19
  553.0 161.4 %all-reduce.5.cloned.1.call-done = (f32[512,512]{1,0:T(8,128)}, f32[512,512]{1,0:T(8,128)}, f32[512,512]{1,0:T(8,128)}, f32[512,512]{1,0:T(8,128)}, f32[512,512]...) async-done(((f32[512,512]{1,0:T(8,128)}, f32[512,512]{1,0:T(8,128)}, f32[512,512]{1,0:T(8,128)}, f32[512,512]{1,0:T(8,128)}, f32[512,512]{1,0:T(8,128)}, ...) | async-done | bytes 13631504 | tf_op jit(solution)/shard_map/psum | solution.py:254
  (430 shorter events, 149.1 us)
Async XLA Ops:
  7.2 192.3 %copy-start = (bf16[512,2048]{1,0:T(8,128)(2,1)S(1)}, bf16[512,2048]{1,0:T(8,128)(2,1)}, u32[]{:S(2)}) copy-start(bf16[512,2048]{1,0:T(8,128)(2,1)} %param.23) | copy-start | bytes 6291460
  7.2 28.8 %copy-start.118 = (s32[2,512]{1,0:T(2,128)S(1)}, s32[2,512]{1,0:T(2,128)}, u32[]{:S(2)}) copy-start(s32[2,512]{1,0:T(2,128)} %param.14) | copy-start | bytes 12292
  7.2 135.5 %all-gather.4.cloned.1.call-start = ((), (), s32[]{:S(2)}) async-start(), calls=%async_computation | async-start | bytes 9437184 | tf_op jit(solution)/shard_map/all_gather | solution.py:134
  8.1 35.0 %copy-start.88 = (f32[512]{0:T(512)}, f32[512]{0:T(512)S(1)}, u32[]{:S(2)}) copy-start(f32[512]{0:T(512)S(1)} %convert_element_type.118) | copy-start | bytes 6148
  9.6 33.5 %copy-start.80 = (f32[2,512]{1,0:T(2,128)}, f32[2,512]{1,0:T(2,128)S(1)}, u32[]{:S(2)}) copy-start(f32[2,512]{1,0:T(2,128)S(1)} %add_rsqrt_fusion.1) | copy-start | bytes 12292
  12.4 30.7 %copy-start.20 = (bf16[2,512,512]{2,1,0:T(8,128)(2,1)S(1)}, bf16[2,512,512]{2,1,0:T(8,128)(2,1)}, u32[]{:S(2)}) copy-start(bf16[2,512,512]{2,1,0:T(8,128)(2,1)} %get-tuple-element.37) | copy-start | bytes 3145732
  12.4 369.5 %all-gather.6.cloned.1.call-start = ((), (), s32[]{:S(2)}) async-start(), calls=%async_computation.1 | async-start | bytes 9437184 | tf_op jit(solution)/shard_map/all_gather | solution.py:214
  36.1 57.3 %copy-start.72 = (pred[128,2]{0,1:T(4,128)(4,1)}, pred[128,2]{0,1:T(4,128)(4,1)S(1)}, u32[]{:S(2)}) copy-start(pred[128,2]{0,1:T(4,128)(4,1)S(1)} %reshape.536) | copy-start | bytes 772
  56.3 58.0 %copy-start.25 = (bf16[2,16,32,8,64]{4,3,2,1,0:T(8,128)(2,1)S(1)}, bf16[2,16,32,8,64]{4,3,2,1,0:T(8,128)(2,1)}, u32[]{:S(2)}) copy-start(bf16[2,16,32,8,64]{4,3,2,1,0:T(8,128)(2,1)} %reshape.514) | copy-start | bytes 3145732
  57.3 33.5 %copy-start.67 = (bf16[2,16,512]{2,1,0:T(8,128)(2,1)}, bf16[2,16,512]{2,1,0:T(8,128)(2,1)S(1)}, u32[]{:S(2)}) copy-start(bf16[2,16,512]{2,1,0:T(8,128)(2,1)S(1)} %multiply_convert_fusion.7) | copy-start | bytes 98308
  90.8 25.3 %copy-start.38 = (bf16[2,128,512]{2,1,0:T(8,128)(2,1)}, bf16[2,128,512]{2,1,0:T(8,128)(2,1)S(1)}, u32[]{:S(2)}) copy-start(bf16[2,128,512]{2,1,0:T(8,128)(2,1)S(1)} %convolution_convert_fusion.7) | copy-start | bytes 786436
  94.1 22.0 %copy-start.24 = (bf16[2,16,32,8,64]{4,3,2,1,0:T(8,128)(2,1)S(1)}, bf16[2,16,32,8,64]{4,3,2,1,0:T(8,128)(2,1)}, u32[]{:S(2)}) copy-start(bf16[2,16,32,8,64]{4,3,2,1,0:T(8,128)(2,1)} %reshape.520) | copy-start | bytes 3145732
  96.5 21.4 %copy-start.41 = (f32[2,128]{1,0:T(2,128)}, f32[2,128]{1,0:T(2,128)S(1)}, u32[]{:S(2)}) copy-start(f32[2,128]{1,0:T(2,128)S(1)} %log_add_fusion.6) | copy-start | bytes 3076
  98.1 19.8 %copy-start.42 = (f32[2,128]{1,0:T(2,128)}, f32[2,128]{1,0:T(2,128)S(1)}, u32[]{:S(2)}) copy-start(f32[2,128]{1,0:T(2,128)S(1)} %add_select_fusion.5) | copy-start | bytes 3076
  99.3 18.7 %copy-start.45 = (f32[2,128]{1,0:T(2,128)}, f32[2,128]{1,0:T(2,128)S(1)}, u32[]{:S(2)}) copy-start(f32[2,128]{1,0:T(2,128)S(1)} %log_add_fusion.5) | copy-start | bytes 3076
  101.0 16.9 %copy-start.58 = (f32[2,128]{1,0:T(2,128)}, f32[2,128]{1,0:T(2,128)S(1)}, u32[]{:S(2)}) copy-start(f32[2,128]{1,0:T(2,128)S(1)} %add_select_fusion.4) | copy-start | bytes 3076
  102.3 15.7 %copy-start.59 = (f32[2,128]{1,0:T(2,128)}, f32[2,128]{1,0:T(2,128)S(1)}, u32[]{:S(2)}) copy-start(f32[2,128]{1,0:T(2,128)S(1)} %log_add_fusion.4) | copy-start | bytes 3076
  104.0 13.9 %copy-start.62 = (f32[2,128]{1,0:T(2,128)}, f32[2,128]{1,0:T(2,128)S(1)}, u32[]{:S(2)}) copy-start(f32[2,128]{1,0:T(2,128)S(1)} %add_select_fusion.3) | copy-start | bytes 3076
  105.3 12.7 %copy-start.63 = (f32[2,128]{1,0:T(2,128)}, f32[2,128]{1,0:T(2,128)S(1)}, u32[]{:S(2)}) copy-start(f32[2,128]{1,0:T(2,128)S(1)} %log_add_fusion.3) | copy-start | bytes 3076
  107.1 10.9 %copy-start.73 = (f32[2,128]{1,0:T(2,128)}, f32[2,128]{1,0:T(2,128)S(1)}, u32[]{:S(2)}) copy-start(f32[2,128]{1,0:T(2,128)S(1)} %add_select_fusion.2) | copy-start | bytes 3076
  108.4 9.5 %copy-start.77 = (f32[2,128]{1,0:T(2,128)}, f32[2,128]{1,0:T(2,128)S(1)}, u32[]{:S(2)}) copy-start(f32[2,128]{1,0:T(2,128)S(1)} %log_add_fusion.2) | copy-start | bytes 3076
  109.7 8.3 %copy-start.115 = (f32[2,128]{1,0:T(2,128)}, f32[2,128]{1,0:T(2,128)S(1)}, u32[]{:S(2)}) copy-start(f32[2,128]{1,0:T(2,128)S(1)} %fusion.79) | copy-start | bytes 3076
  110.4 7.6 %copy-start.78 = (f32[2,128]{1,0:T(2,128)}, f32[2,128]{1,0:T(2,128)S(1)}, u32[]{:S(2)}) copy-start(f32[2,128]{1,0:T(2,128)S(1)} %add_select_fusion.1) | copy-start | bytes 3076
  161.0 10.0 %copy-start.14 = (bf16[2,16,16384]{2,1,0:T(8,128)(2,1)}, bf16[2,16,16384]{2,1,0:T(8,128)(2,1)S(1)}, u32[]{:S(2)}) copy-start(bf16[2,16,16384]{2,1,0:T(8,128)(2,1)S(1)} %convolution_convert_fusion) | copy-start | bytes 3145732
  178.4 7.8 %copy-start.26 = (bf16[2,16,32,8,64]{4,3,2,1,0:T(8,128)(2,1)S(1)}, bf16[2,16,32,8,64]{4,3,2,1,0:T(8,128)(2,1)}, u32[]{:S(2)}) copy-start(bf16[2,16,32,8,64]{4,3,2,1,0:T(8,128)(2,1)} %reshape.518) | copy-start | bytes 3145732
  190.7 6.5 copy-start.6
  199.4 13.3 %copy-start.4 = (f32[2,512,512]{2,1,0:T(8,128)}, f32[2,512,512]{2,1,0:T(8,128)S(1)}, u32[]{:S(2)}) copy-start(f32[2,512,512]{2,1,0:T(8,128)S(1)} %get-tuple-element.49) | copy-start | bytes 6291460
  199.5 13.3 %copy-start.69 = (f32[2,512]{1,0:T(2,128)}, f32[2,512]{1,0:T(2,128)S(1)}, u32[]{:S(2)}) copy-start(f32[2,512]{1,0:T(2,128)S(1)} %add_rsqrt_fusion) | copy-start | bytes 12292
  202.1 7.4 %copy-start.22 = (f32[2,512,2048]{2,1,0:T(8,128)}, f32[2,512,2048]{2,1,0:T(8,128)S(1)}, u32[]{:S(2)}) copy-start(f32[2,512,2048]{2,1,0:T(8,128)S(1)} %fusion.30) | copy-start | bytes 25165828
  219.6 8.2 %copy-start.3 = (f32[2,16,8,32,64]{4,3,2,1,0:T(8,128)S(1)}, f32[2,16,8,32,64]{4,3,2,1,0:T(8,128)}, u32[]{:S(2)}) copy-start(f32[2,16,8,32,64]{4,3,2,1,0:T(8,128)} %copy-done.2) | copy-start | bytes 6291460
  219.6 8.2 %copy-start.17 = (bf16[2,16,64,8,64]{4,2,3,1,0:T(8,128)(2,1)S(1)}, bf16[2,16,64,8,64]{4,2,3,1,0:T(8,128)(2,1)}, u32[]{:S(2)}) copy-start(bf16[2,16,64,8,64]{4,2,3,1,0:T(8,128)(2,1)} %copy-done.16) | copy-start | bytes 6291460
  219.6 8.1 %copy-start.37 = (pred[2,16,32,64]{3,2,1,0:T(8,128)(4,1)S(1)}, pred[2,16,32,64]{3,2,1,0:T(8,128)(4,1)}, u32[]{:S(2)}) copy-start(pred[2,16,32,64]{3,2,1,0:T(8,128)(4,1)} %concatenate.11) | copy-start | bytes 196612
  219.6 8.1 %copy-start.43 = (f32[2,16,8,32]{3,2,1,0:T(8,128)S(1)}, f32[2,16,8,32]{3,2,1,0:T(8,128)}, u32[]{:S(2)}) copy-start(f32[2,16,8,32]{3,2,1,0:T(8,128)} %log_add_fusion) | copy-start | bytes 98308
  241.8 10.0 %copy-start.9 = (bf16[2,16,32,8,64]{4,3,2,1,0:T(8,128)(2,1)}, bf16[2,16,32,8,64]{4,3,2,1,0:T(8,128)(2,1)S(1)}, u32[]{:S(2)}) copy-start(bf16[2,16,32,8,64]{4,3,2,1,0:T(8,128)(2,1)S(1)} %copy.78) | copy-start | bytes 3145732
  254.1 50.8 %copy-start.8 = (bf16[2,16,32,8,64]{4,3,2,1,0:T(8,128)(2,1)S(1)}, bf16[2,16,32,8,64]{4,3,2,1,0:T(8,128)(2,1)}, u32[]{:S(2)}) copy-start(bf16[2,16,32,8,64]{4,3,2,1,0:T(8,128)(2,1)} %copy.70) | copy-start | bytes 3145732
  257.0 457.4 %all-reduce.5.cloned.1.call-start = ((), (), s32[]{:S(2)}) async-start(), calls=%async_computation.2 | async-start | bytes 27262976 | tf_op jit(solution)/shard_map/psum | solution.py:254
  318.3 13.3 %copy-start.7 = (bf16[2,16,32,8,64]{4,3,2,1,0:T(8,128)(2,1)}, bf16[2,16,32,8,64]{4,3,2,1,0:T(8,128)(2,1)S(1)}, u32[]{:S(2)}) copy-start(bf16[2,16,32,8,64]{4,3,2,1,0:T(8,128)(2,1)S(1)} %copy.72) | copy-start | bytes 3145732
  342.5 6.7 slice-start.2
  435.3 30.0 %copy-start.68 = (bf16[2,16,512]{2,1,0:T(8,128)(2,1)S(1)}, bf16[2,16,512]{2,1,0:T(8,128)(2,1)}, u32[]{:S(2)}) copy-start(bf16[2,16,512]{2,1,0:T(8,128)(2,1)} %copy-done.67) | copy-start | bytes 98308
  481.2 6.9 copy-start.124
  484.8 10.7 %slice-start = ((s8[8388608]{0:T(1024)(128)(4,1)}), s8[4194304]{0:T(1024)(128)(4,1)S(1)}, s32[]{:S(2)}) async-start(s8[8388608]{0:T(1024)(128)(4,1)} %bitcast.190), calls=%async_computation.3 | async-start | bytes 8388608
  488.1 7.4 %slice-start.1 = ((s8[8388608]{0:T(1024)(128)(4,1)}), s8[4194304]{0:T(1024)(128)(4,1)S(1)}, s32[]{:S(2)}) async-start(s8[8388608]{0:T(1024)(128)(4,1)} %bitcast.190), calls=%async_computation.4 | async-start | bytes 8388608
  488.1 7.4 %copy-start.64 = (bf16[2,128,128]{2,1,0:T(8,128)(2,1)S(1)}, bf16[2,128,128]{2,1,0:T(8,128)(2,1)}, u32[]{:S(2)}) copy-start(bf16[2,128,128]{2,1,0:T(8,128)(2,1)} %get-tuple-element.34) | copy-start | bytes 196612
  502.7 6.5 copy-start.119
  502.7 46.4 %copy-start.71 = (f32[2,512]{1,0:T(2,128)S(1)}, f32[2,512]{1,0:T(2,128)}, u32[]{:S(2)}) copy-start(f32[2,512]{1,0:T(2,128)} %copy-done.69) | copy-start | bytes 12292
  502.7 46.4 %copy-start.76 = (f32[512]{0:T(512)S(1)}, f32[512]{0:T(512)}, u32[]{:S(2)}) copy-start(f32[512]{0:T(512)} %convert_element_type.134) | copy-start | bytes 6148
  502.7 46.4 %copy-start.87 = (f32[2,512]{1,0:T(2,128)S(1)}, f32[2,512]{1,0:T(2,128)}, u32[]{:S(2)}) copy-start(f32[2,512]{1,0:T(2,128)} %copy-done.86) | copy-start | bytes 12292
  714.4 6.8 copy-start.51
  (84 other events, 237.6 us)
Sparse Core Ops, SparseCore 0:
  12.5 130.1 all-gather.3
  257.1 124.7 all-gather.5
  466.8 247.6 all-reduce.4
where the time goes:
time: 743 us; the launch traced here: 736 us
  waiting for transfers between devices  214 us (29%)
  blocking collectives  168 us (23%)
  local copies, waits for them, and re-layouts  155 us (21%)
  matrix products  118 us (16%)
  other arithmetic  61.8 us (8%)
  between operations  18.8 us (3%)
    psum x1, waiting for transfers between devices, body(): lax.psum((grad_gain_one, grad_query, grad_key, grad_value, grad_output, g...  161 us
    psum x1, blocking collectives, body(): block_grand_total = lax.psum(count_mine, ('dp', 'seq'))  42.5 us
    psum x1, blocking collectives, body(): lax.psum((grad_gain_one, grad_query, grad_key, grad_value, grad_output, g...  38.5 us
    all_gather x1, blocking collectives, body(): lax.all_gather(found_grads.astype(jnp.bfloat16), 'seq', axis=2, tiled=True)  32.4 us
    all_gather x1, blocking collectives, body(): lax.all_gather(summary, 'seq', axis=1, tiled=True)  32.2 us
    dot_general x9, matrix products, product_back(): lax.dot_general(left_mat, right_mat, (((left_mat.ndim - 1,), (1,)), ((),...  32 us
    unnamed x268, local copies, waits for them, and re-layouts  31.9 us
    all_gather x1, waiting for transfers between devices, body(): shard_piece = lax.all_gather(mixed_gradient, 'seq', axis=1, tiled=True)  28 us
  transfers between devices with their start and end apart: 3, of which 3 were waited for; matrix products, arithmetic and copies ran while one was open for 19% of the time, Pallas kernels for 0%

commit v1 on v0

--- a/solution.py
+++ b/solution.py
@@ -76,6 +76,68 @@
     same_seg = segments[:, :, :, None] == segments[:, :, None, :]
     allowed = jnp.concatenate([same_seg, jnp.ones_like(same_seg)], axis=-1)[:, :, None]
     return jnp.where(allowed, scores, NEG)
+
+
+def bits(size):
+    return [1 << k for k in range(size.bit_length() - 1)]
+
+
+def swap(array, axis, bit):
+    return lax.ppermute(array, axis, [(i, i ^ bit) for i in range(lax.axis_size(axis))])
+
+
+def reduce_all(rows, order):
+    for axis, bit in order:
+        halves = rows.reshape(2, rows.shape[0] // 2, rows.shape[1])
+        mine = (lax.axis_index(axis) // bit) % 2
+        keep = lax.dynamic_index_in_dim(halves, mine, 0, False)
+        give = lax.dynamic_index_in_dim(halves, 1 - mine, 0, False)
+        got = swap(give, axis, bit)
+        rows = (keep.astype(jnp.float32) + got.astype(jnp.float32)).astype(jnp.bfloat16)
+    for axis, bit in reversed(order):
+        mine = (lax.axis_index(axis) // bit) % 2
+        got = swap(rows, axis, bit)
+        both = jnp.where(mine == 0, jnp.stack([rows, got]), jnp.stack([got, rows]))
+        rows = both.reshape(2 * rows.shape[0], rows.shape[1])
+    return rows
+
+
+def sum_seq(part):
+    parts = lax.axis_size("seq")
+    if parts * part.size > 1 << 20:
+        return lax.psum(part.astype(jnp.float32), "seq")
+    heard = lax.all_to_all(
+        jnp.broadcast_to(part[None], (parts,) + part.shape), "seq", 0, 0, tiled=True
+    )
+    return jnp.sum(heard.astype(jnp.float32), axis=0)
+
+
+def to_chunks(blocks, parts):
+    seqs, count, rows, width = blocks.shape
+    row_parts = min(parts, rows)
+    col_parts = parts // row_parts
+    cut = blocks.reshape(
+        seqs, count, row_parts, rows // row_parts, col_parts, width // col_parts
+    ).transpose(2, 4, 0, 3, 1, 5)
+    return cut.reshape(parts, seqs, rows // row_parts, count, width // col_parts)
+
+
+def from_chunks(chunks):
+    parts, seqs, rows, count, width = chunks.shape
+    row_parts = min(parts, BLOCK)
+    col_parts = parts // row_parts
+    cut = chunks.reshape(row_parts, col_parts, seqs, rows, count, width).transpose(2, 4, 0, 3, 1, 5)
+    return cut.reshape(seqs, count, row_parts * rows, col_parts * width)
+
+
+def gathered(chunks):
+    parts, seqs, rows, count, width = chunks.shape
+    return chunks.transpose(1, 2, 0, 3, 4).reshape(seqs, rows, parts * count, width)
+
+
+def scattered(spread, parts):
+    seqs, rows, count, width = spread.shape
+    return spread.reshape(seqs, rows, parts, count // parts, width).transpose(2, 0, 1, 3, 4)
 
 
 def body(
@@ -99,9 +161,9 @@
     flat_width = BLOCK * model_width
     att_scale = 1.0 / math.sqrt(head_dim)
     sort_scale = SORT_GAIN * BLOCK / math.sqrt(model_width)
-    first_block = lax.axis_index("seq") * local_blocks
-    count_mine = jnp.sum(real_block).astype(jnp.float32)
-    block_grand_total = lax.psum(count_mine, ("dp", "seq"))
+    seq_size = lax.axis_size("seq")
+    seq_index = lax.axis_index("seq")
+    first_block = seq_index * local_blocks
     inputs_f = inputs.astype(jnp.float32)
     gain_one = gain_attn.astype(jnp.float32)
     gain_two = gain_ffn.astype(jnp.float32)
@@ -110,11 +172,23 @@
     blocks = hidden.reshape(seq_count, local_blocks, BLOCK, model_width)
     blocks_flat = blocks.reshape(seq_count, local_blocks, flat_width)
     summary = jnp.mean(blocks, axis=2, dtype=jnp.float32).astype(jnp.bfloat16)
-    summary_all, real_all = (
-        lax.all_gather(summary, "seq", axis=1, tiled=True),
-        lax.all_gather(real_block.astype(jnp.bfloat16), "seq", axis=1, tiled=True),
-    )
+    flag_rows = jnp.broadcast_to(
+        real_block.astype(jnp.bfloat16)[:, :, None], (seq_count, local_blocks, 128)
+    )
+    told = jnp.concatenate([summary, flag_rows], axis=-1)
+    told_all = lax.all_to_all(
+        jnp.broadcast_to(told[None], (seq_size,) + told.shape), "seq", 0, 0, tiled=True
+    )
+    told_all = told_all.transpose(1, 0, 2, 3).reshape(seq_count, seq_size * local_blocks, -1)
+    summary_all = told_all[:, :, :model_width]
+    real_all = told_all[:, :, model_width]
     retained_target_slots = real_all == 1
+    block_grand_total = jnp.sum(real_all.astype(jnp.float32)).reshape(1, 1)
+    for bit in bits(lax.axis_size("dp")):
+        block_grand_total = block_grand_total + swap(block_grand_total, "dp", bit)
+    block_grand_total = block_grand_total[0, 0]
+    spread = lax.all_to_all(to_chunks(blocks, seq_size), "seq", 0, 0, tiled=True)
+    spread = gathered(spread)
     sort_proj = product(summary_all, w_sort).astype(jnp.bfloat16)
     permutation_raw_scores = sort_scale * jnp.einsum(
         "sid,sjd->sij", sort_proj, summary_all, preferred_element_type=jnp.float32
@@ -130,14 +204,12 @@
         jnp.where((real_block == 1)[:, :, None], jnp.exp(plan_rows) * plan_rows, 0.0)
     )
     prob_low = prob_full.astype(jnp.bfloat16)
-    prob_rows = lax.dynamic_slice_in_dim(prob_low, first_block, local_blocks, 1)
-    shard_piece = lax.all_gather(blocks, "seq", axis=1, tiled=True)
-    flat_piece = shard_piece.reshape(seq_count, shard_piece.shape[1], flat_width)
-    prob_part = prob_rows
-    mixed_sum = jnp.einsum(
-        "sim,smf->sif", prob_part, flat_piece, preferred_element_type=jnp.float32
-    )
-    mixed = mixed_sum.astype(jnp.bfloat16).reshape(seq_count, local_blocks, BLOCK, model_width)
+    mixed_spread = jnp.einsum(
+        "sim,stmf->stif", prob_low, spread, preferred_element_type=jnp.float32
+    ).astype(jnp.bfloat16)
+    mixed = from_chunks(
+        lax.all_to_all(scattered(mixed_spread, seq_size), "seq", 0, 0, tiled=True)
+    )
     shape_heads = (seq_count, local_blocks, BLOCK, HEADS, head_dim)
     queries = product(hidden, w_query).astype(jnp.bfloat16).reshape(shape_heads)
     key_local = product(hidden, w_key).astype(jnp.bfloat16).reshape(shape_heads)
@@ -167,7 +239,13 @@
     grad_out = weight_grad(activation_low, cotangent)
     (d_pre,) = gelu_back(product_back(cotangent, w_out))
     d_pre_low = d_pre.astype(jnp.bfloat16)
-    grad_in = weight_grad(hidden_two, d_pre_low)
+    grad_in = jnp.concatenate(
+        [
+            weight_grad(hidden_two, d_pre_low[..., c : c + model_width])
+            for c in range(0, d_pre_low.shape[-1], model_width)
+        ],
+        axis=0,
+    )
     d_resid, grad_gain_two = norm_back(product_back(d_pre_low, w_in), unit_two, scale_two, gain_two)
     d_resid = d_resid + cotangent.astype(jnp.float32)
     d_branch = d_resid.astype(jnp.bfloat16)
@@ -210,19 +288,19 @@
     mixed_gradient = (
         product_back(d_key_sorted, w_key) + product_back(d_value_sorted, w_value)
     ).astype(jnp.bfloat16)
-    prob_cols = lax.dynamic_slice_in_dim(prob_low, first_block, local_blocks, 2)
-    shard_piece = lax.all_gather(mixed_gradient, "seq", axis=1, tiled=True)
-    flat_piece = shard_piece.reshape(seq_count, shard_piece.shape[1], flat_width)
-    prob_part = prob_cols
+    dmixed_spread = gathered(
+        lax.all_to_all(to_chunks(mixed_gradient, seq_size), "seq", 0, 0, tiled=True)
+    )
+    d_prob = jnp.einsum(
+        "stmf,stjf->smj", dmixed_spread, spread, preferred_element_type=jnp.float32
+    ).astype(jnp.bfloat16)
+    d_prob = sum_seq(d_prob)
     block_sum = jnp.einsum(
-        "smj,smf->sjf", prob_part, flat_piece, preferred_element_type=jnp.float32
-    )
-    found_grads = jnp.einsum(
-        "smf,sjf->smj", flat_piece, blocks_flat, preferred_element_type=jnp.float32
-    )
-    d_prob = lax.all_gather(found_grads.astype(jnp.bfloat16), "seq", axis=2, tiled=True).astype(
-        found_grads.dtype
-    )
+        "smj,stmf->stjf", prob_low, dmixed_spread, preferred_element_type=jnp.float32
+    ).astype(jnp.bfloat16)
+    block_sum = from_chunks(
+        lax.all_to_all(scattered(block_sum, seq_size), "seq", 0, 0, tiled=True)
+    ).astype(jnp.float32)
     entropy_grad = jnp.where(
         retained_target_slots[:, :, None], prob_full * logarithmic_coupling_matrix + prob_full, 0.0
     )
@@ -241,7 +319,7 @@
     ) + product_back(d_proj, w_sort)
     d_hidden = (
         d_hidden.reshape(seq_count, local_blocks, BLOCK, model_width)
-        + block_sum.reshape(seq_count, local_blocks, BLOCK, model_width)
+        + block_sum
         + d_summary[:, :, None, :] / BLOCK
     )
     d_input, grad_gain_one = norm_back(
@@ -251,23 +329,46 @@
         gain_one,
     )
     input_grad = (d_input + d_resid).astype(jnp.bfloat16)
-    totals = lax.psum(
-        (
-            grad_gain_one,
-            grad_query,
-            grad_key,
-            grad_value,
-            grad_output,
-            grad_sort,
-            grad_gain_two,
-            grad_in,
-            grad_out,
-            entropy_mine,
-        ),
+    dp_size = lax.axis_size("dp")
+    dp_bits, seq_bits = bits(dp_size), bits(seq_size)
+    one = [("dp", bit) for bit in dp_bits] + [("seq", bit) for bit in seq_bits]
+    two = one[:1] + [one[len(dp_bits)]] + one[1 : len(dp_bits)] + one[len(dp_bits) + 1 :]
+    grad_out = reduce_all(grad_out.astype(jnp.bfloat16), one).astype(jnp.float32)
+    grad_in = reduce_all(grad_in.astype(jnp.bfloat16), two)
+    grad_in = jnp.concatenate(
+        [grad_in[c : c + model_width] for c in range(0, grad_in.shape[0], model_width)], axis=1
+    ).astype(jnp.float32)
+    late = jnp.concatenate([grad_query, grad_key, grad_value, grad_output], axis=0)
+    late = reduce_all(late.astype(jnp.bfloat16), one).astype(jnp.float32)
+    grad_query, grad_key, grad_value, grad_output = jnp.split(late, 4, axis=0)
+    grad_sort = reduce_all(grad_sort.astype(jnp.bfloat16), two).astype(jnp.float32)
+    small = jnp.stack(
+        [grad_gain_one, grad_gain_two, jnp.full_like(grad_gain_one, entropy_mine)]
+        + [jnp.zeros_like(grad_gain_one)] * 5
+    )
+    small = lax.all_to_all(
+        jnp.broadcast_to(small[None], (dp_size * seq_size,) + small.shape),
         ("dp", "seq"),
-    )
-    penalty = -totals[9] / block_grand_total
-    return (output, input_grad, penalty) + tuple(totals[:9])
+        0,
+        0,
+        tiled=True,
+    )
+    small = jnp.sum(small, axis=0)
+    penalty = -small[2, 0] / block_grand_total
+    return (
+        output,
+        input_grad,
+        penalty,
+        small[0],
+        grad_query,
+        grad_key,
+        grad_value,
+        grad_output,
+        grad_sort,
+        small[1],
+        grad_in,
+        grad_out,
+    )
 
 
 def solution(mesh):

time: 743 us -> 467 us (0.63)
  blocking collectives: 168 us -> 0 us
  waiting for transfers between devices: 214 us -> 67.1 us
  starting transfers between devices: 0.12 us -> 86.3 us
  matrix products: 118 us -> 98.3 us
  local copies, waits for them, and re-layouts: 155 us -> 139 us
  between operations: 18.8 us -> 7.09 us
    psum x1 -> x0, waiting for transfers between devices: 161 us -> none  [body(): lax.psum((grad_gain_one, grad_query, grad_key, grad_value, grad_output, g...]
    all_gather x3 -> x0, blocking collectives: 86.8 us -> none  [the longest x1 32.4 us: body(): lax.all_gather(found_grads.astype(jnp.bfloat16), 'seq', axis=2, tiled=True)]
    psum x2 -> x0, blocking collectives: 81 us -> none  [the longest x1 42.5 us: body(): block_grand_total = lax.psum(count_mine, ('dp', 'seq'))]
    ppermute x0 -> x42, waiting for transfers between devices: none -> 61.8 us  [swap(): lax.ppermute(array, axis, [(i, i ^ bit) for i in range(lax.axis_size(axis...]
    all_gather x2 -> x0, waiting for transfers between devices: 52.7 us -> none  [the longest x1 28 us: body(): shard_piece = lax.all_gather(mixed_gradient, 'seq', axis=1, tiled=True)]
    ppermute x0 -> x42, starting transfers between devices: none -> 49.3 us  [swap(): lax.ppermute(array, axis, [(i, i ^ bit) for i in range(lax.axis_size(axis...]
    all_to_all x0 -> x7, starting transfers between devices: none -> 37 us  [the longest x1 7.28 us: body(): lax.all_to_all(jnp.broadcast_to(told[None], (seq_size,) + told.shape), 's...]
    reshape x3 -> x5, local copies, waits for them, and re-layouts: 30 us -> 7.59 us  [the longest x2 3.69 us: scattered(): spread.reshape(seqs, rows, parts, count // parts, width)]
  transfers between devices with their start and end apart: 3 -> 49, of which waited for: 3 -> 21; matrix products, arithmetic and copies ran while one was open for 19% -> 28% of each run, Pallas kernels for 0% -> 0%
where the time goes in v1:
time: 467 us; the launch traced here: 461 us
  local copies, waits for them, and re-layouts  139 us (30%)
  matrix products  98.3 us (21%)
  starting transfers between devices  86.3 us (18%)
  waiting for transfers between devices  67.1 us (14%)
  other arithmetic  63.7 us (14%)
  between operations  7.09 us (2%)
    ppermute x42, waiting for transfers between devices, swap(): lax.ppermute(array, axis, [(i, i ^ bit) for i in range(lax.axis_size(axis...  61.8 us
    ppermute x42, starting transfers between devices, swap(): lax.ppermute(array, axis, [(i, i ^ bit) for i in range(lax.axis_size(axis...  49.3 us
    dot_general x9, matrix products, product_back(): lax.dot_general(left_mat, right_mat, (((left_mat.ndim - 1,), (1,)), ((),...  27.2 us
    unnamed x260, local copies, waits for them, and re-layouts  23 us
    dot_general x9, matrix products, product(): lax.dot_general(left_mat, right_mat, (((left_mat.ndim - 1,), (0,)), ((),...  22.9 us
    dot_general x12, matrix products, weight_grad(): lax.dot_general(flat_left, flat_right, (((0,), (0,)), ((), ())), preferre...  20.6 us
    another operation x5, local copies, waits for them, and re-layouts, weight_grad(): flat_right = right_mat.reshape(-1, right_mat.shape[-1])  14.3 us
    select_n x20, other arithmetic, reduce_all(): both = jnp.where(mine == 0, jnp.stack([rows, got]), jnp.stack([got, rows]))  12.8 us
  transfers between devices with their start and end apart: 49, of which 21 were waited for; matrix products, arithmetic and copies ran while one was open for 28% of the time, Pallas kernels for 0%

profile of v1, /device:TPU:0, one launch (start us, length us, event | category | flops | bytes accessed | tf_op | source)
XLA Modules:
  0.0 461.3 jit_solution(5577868108244137616)
XLA Ops:
  6.6 7.3 %all-to-all-start.1 = ((bf16[8,2,16,640]{3,2,1,0:T(8,128)(2,1)}), bf16[8,2,16,640]{3,2,1,0:T(8,128)(2,1)}, u32[]{:S(2)}, u32[]{:S(2)}) async-start(bf16[8,2,16,640]{3,2,1,0:T(8,128)(2,1)} %broadcast_in_dim.113), calls=%async_computation.1 | async-start | bytes 655360 | tf_op jit(solution)/shard_map/all_to_all | solution.py:179
  17.8 3.9 reshape.1181
  24.4 6.2 %all-to-all-start = ((bf16[8,2,4,16,512]{4,3,2,1,0:T(8,128)(2,1)}), bf16[8,2,4,16,512]{4,3,2,1,0:T(8,128)(2,1)S(1)}, u32[]{:S(2)}, u32[]{:S(2)}) async-start(bf16[8,2,4,16,512]{4,3,2,1,0:T(8,128)(2,1)} %bitcast.421), calls=%async_computation | async-start | bytes 2097152 | tf_op jit(solution)/shard_map/all_to_all | solution.py:190
  50.7 5.3 %all-to-all-done = bf16[8,2,4,16,512]{4,3,2,1,0:T(8,128)(2,1)S(1)} async-done(((bf16[8,2,4,16,512]{4,3,2,1,0:T(8,128)(2,1)}), bf16[8,2,4,16,512]{4,3,2,1,0:T(8,128)(2,1)S(1)}, u32[]{:S(2)}, u32[]{:S(2)}) %all-to-all-start) | async-done | bytes 1048608 | tf_op jit(solution)/shard_map/all_to_all | solution.py:190
  60.6 4.5 all-to-all-start.2
  65.1 3.0 convolution_convert_fusion.5
  68.1 4.0 reshape.1180
  74.9 3.9 reshape.1172
  79.1 3.5 copy_dynamic-update-slice_fusion.3
  88.6 2.9 collective-permute-start.1
  96.8 3.1 convolution_convert_fusion.3
  101.6 4.0 reshape.1179
  107.7 3.5 copy_dynamic-update-slice_fusion
  111.2 4.7 %fusion.13 = (f32[2,16,8,32]{3,2,1,0:T(8,128)S(1)}, f32[2,16,8,32,64]{4,3,2,1,0:T(8,128)S(1)}) fusion(pred[2,16,32,64]{3,2,1,0:T(8,128)(4,1)S(1)} %concatenate.26, bf16[2,16,64,8,64]{4,2,3,1,0:T(8,128)(2,1)} %copy_dynamic-update-slice_fusion, bf16[2,16,32,8,64]{4,3,2,1,0:T(8,128)(2,1)S(1)} %copy-done.8), kind=kOutput, calls=%fused_computation.29 | convolution fusion | flops 68673536 | bytes 5341184 | tf_op jit(solution)/shard_map/snthd,snkhd->snhtk/dot_general | solution.py:73
  120.5 3.4 convert_bitcast_fusion.2
  126.2 4.0 reshape_reshape.32
  130.3 4.1 reshape.1183
  139.2 3.8 add_convert_fusion.1
  143.0 4.4 bitcast_convert_fusion
  147.4 7.5 %fusion.6 = bf16[2,512,2048]{2,1,0:T(8,128)(2,1)S(1)} fusion(f32[2,512,2048]{2,1,0:T(8,128)S(1)} %fusion.33, bf16[2,512,512]{2,1,0:T(8,128)(2,1)S(1)} %copy-done.31, bf16[2048,512]{1,0:T(8,128)(2,1)S(1)} %copy-done.125), kind=kOutput, calls=%fused_computation.8 | convolution fusion | flops 2189426688 | bytes 15728640 | tf_op jit(solution)/shard_map/dot_general | solution.py:55
  161.1 3.2 multiply_reduce_fusion.1
  171.1 8.1 %convert_bitcast_fusion = bf16[2,16,64,8,64]{4,2,3,1,0:T(8,128)(2,1)} fusion(bf16[2,16,32,8,64]{4,3,2,1,0:T(8,128)(2,1)S(1)} %reshape.1184, f32[2,16,8,32,64]{4,3,2,1,0:T(8,128)} %copy-done.2, f32[2,16,8,32]{3,2,1,0:T(8,128)} %copy-done.63, f32[2,16,8,32]{3,2,1,0:T(8,128)} %copy-done.46, pred[2,16,32,64]{3,2,1,0:T(8,128)(4,1)S(1)} %concatenate.26), kind=kOutput, calls=%fused_computation.13 | convolution fusion | flops 70778880 | bytes 5373952 | tf_op jit(solution)/shard_map/snhtk,snthd->snkhd/dot_general | solution.py:270
  179.2 3.2 multiply_reduce_fusion
  187.7 3.6 fusion.7
  198.6 4.5 fusion.150
  216.0 4.0 reshape_reshape.30
  220.0 4.0 reshape_reshape.27
  224.1 3.4 fusion.155
  248.2 4.0 reshape.1187
  252.2 4.2 reshape.1186
  261.3 6.0 %all-to-all-start.3 = ((bf16[8,2,4,16,512]{4,2,3,1,0:T(4,128)(2,1)}), bf16[8,2,4,16,512]{4,2,3,1,0:T(4,128)(2,1)}, u32[]{:S(2)}, u32[]{:S(2)}) async-start(bf16[8,2,4,16,512]{4,2,3,1,0:T(4,128)(2,1)} %bitcast.419), calls=%async_computation.3 | async-start | bytes 2097152 | tf_op jit(solution)/shard_map/all_to_all | solution.py:292
  267.4 3.3 fusion.73
  280.6 8.7 %collective-permute-done.33 = bf16[512,512]{1,0:T(8,128)(2,1)S(1)} collective-permute-done((bf16[512,512]{1,0:T(8,128)(2,1)S(1)}, bf16[512,512]{1,0:T(8,128)(2,1)S(1)}, u32[]{:S(2)}, u32[]{:S(2)}) %collective-permute-start.33) | collective-permute-done | bytes 524320 | tf_op jit(solution)/shard_map/ppermute | solution.py:86
  291.5 3.8 collective-permute-done.23
  296.6 4.0 collective-permute-done.3
  313.6 4.5 all-to-all-start.5
  326.3 4.1 collective-permute-done.5
  330.5 5.2 %collective-permute-start.6 = (bf16[64,512]{1,0:T(8,128)(2,1)S(1)}, bf16[64,512]{1,0:T(8,128)(2,1)S(1)}, u32[]{:S(2)}, u32[]{:S(2)}) collective-permute-start(bf16[64,512]{1,0:T(8,128)(2,1)S(1)} %dynamic-slice_bitcast_fusion.17), channel_id=1, source_target_pairs={{0,4},{1,5},{2,6},{3,7},{4,0},{5,1},{6,2},{7,3},{8,12},{9,13},{10,... | collective-permute-start | bytes 196616 | tf_op jit(solution)/shard_map/ppermute | solution.py:86
  335.7 4.5 collective-permute-done.36
  340.3 3.4 collective-permute-done.26
  349.8 4.5 all-to-all-start.4
  367.7 3.8 collective-permute-done.8
  380.5 9.0 %collective-permute-done.14 = bf16[64,512]{1,0:T(8,128)(2,1)S(1)} collective-permute-done((bf16[64,512]{1,0:T(8,128)(2,1)S(1)}, bf16[64,512]{1,0:T(8,128)(2,1)S(1)}, u32[]{:S(2)}, u32[]{:S(2)}) %collective-permute-start.14) | collective-permute-done | bytes 65568 | tf_op jit(solution)/shard_map/ppermute | solution.py:86
  412.8 3.6 collective-permute-done.20
  420.0 3.0 reshape.1216
  423.0 6.0 %fusion.20 = (f32[512]{0:T(512)S(1)}, f32[2,512]{1,0:T(2,128)S(1)}, f32[2,512,512]{2,1,0:T(8,128)}) fusion(bf16[2,512,512]{2,1,0:T(8,128)(2,1)S(1)} %copy-done.6, f32[2,512]{1,0:T(2,128)S(1)} %copy-done.73, f32[512]{0:T(512)S(1)} %copy-done.79, f32[2,16,512]{2,1,0:T(8,128)S(1)} %copy-done.71, f32[2,512,512]{2,1,0:T(8,128)} %reshape.1216, ...), kind=kOutput, calls=%fused_computation.36 | convolution fusion | flops 542636544 | bytes 11087872 | tf_op jit(solution)/shard_map/dot_general | solution.py:55
  430.5 4.1 all-to-all-start.6
  434.6 3.9 fusion.19
  (596 shorter events, 239.6 us)
Async XLA Ops:
  6.6 17.9 %all-to-all-start.1 = ((bf16[8,2,16,640]{3,2,1,0:T(8,128)(2,1)}), bf16[8,2,16,640]{3,2,1,0:T(8,128)(2,1)}, u32[]{:S(2)}, u32[]{:S(2)}) async-start(bf16[8,2,16,640]{3,2,1,0:T(8,128)(2,1)} %broadcast_in_dim.113), calls=%async_computation.1 | async-start | bytes 655360 | tf_op jit(solution)/shard_map/all_to_all | solution.py:179
  24.4 31.6 %all-to-all-start = ((bf16[8,2,4,16,512]{4,3,2,1,0:T(8,128)(2,1)}), bf16[8,2,4,16,512]{4,3,2,1,0:T(8,128)(2,1)S(1)}, u32[]{:S(2)}, u32[]{:S(2)}) async-start(bf16[8,2,4,16,512]{4,3,2,1,0:T(8,128)(2,1)} %bitcast.421), calls=%async_computation | async-start | bytes 2097152 | tf_op jit(solution)/shard_map/all_to_all | solution.py:190
  60.6 32.2 %all-to-all-start.2 = ((bf16[8,2,4,16,512]{4,2,3,1,0:T(4,128)(2,1)}), bf16[8,2,4,16,512]{4,2,3,1,0:T(4,128)(2,1)}, u32[]{:S(2)}, u32[]{:S(2)}) async-start(bf16[8,2,4,16,512]{4,2,3,1,0:T(4,128)(2,1)} %bitcast.435), calls=%async_computation.2 | async-start | bytes 2097152 | tf_op jit(solution)/shard_map/all_to_all | solution.py:211
  88.6 3.6 collective-permute-start.1
  237.6 35.1 %collective-permute-start.32 = (bf16[1024,512]{1,0:T(8,128)(2,1)}, bf16[1024,512]{1,0:T(8,128)(2,1)}, u32[]{:S(2)}, u32[]{:S(2)}) collective-permute-start(bf16[1024,512]{1,0:T(8,128)(2,1)} %dynamic-slice_bitcast_fusion), channel_id=1, source_target_pairs={{0,8},{8,0},{16,24},{24,16},{1,9},{9,1},{17,25},{25,17},{2,10},{10... | collective-permute-start | bytes 3145736 | tf_op jit(solution)/shard_map/ppermute | solution.py:86
  237.6 38.4 %collective-permute-start.22 = (bf16[1024,512]{1,0:T(8,128)(2,1)}, bf16[1024,512]{1,0:T(8,128)(2,1)}, u32[]{:S(2)}, u32[]{:S(2)}) collective-permute-start(bf16[1024,512]{1,0:T(8,128)(2,1)} %dynamic-slice_bitcast_fusion.1), channel_id=1, source_target_pairs={{0,8},{8,0},{16,24},{24,16},{1,9},{9,1},{17,25},{25,17},{2,10},{10... | collective-permute-start | bytes 3145736 | tf_op jit(solution)/shard_map/ppermute | solution.py:86
  261.3 47.1 %all-to-all-start.3 = ((bf16[8,2,4,16,512]{4,2,3,1,0:T(4,128)(2,1)}), bf16[8,2,4,16,512]{4,2,3,1,0:T(4,128)(2,1)}, u32[]{:S(2)}, u32[]{:S(2)}) async-start(bf16[8,2,4,16,512]{4,2,3,1,0:T(4,128)(2,1)} %bitcast.419), calls=%async_computation.3 | async-start | bytes 2097152 | tf_op jit(solution)/shard_map/all_to_all | solution.py:292
  267.3 12.4 %collective-permute-start.2 = (bf16[1024,512]{1,0:T(8,128)(2,1)}, bf16[1024,512]{1,0:T(8,128)(2,1)S(1)}, u32[]{:S(2)}, u32[]{:S(2)}) collective-permute-start(bf16[1024,512]{1,0:T(8,128)(2,1)} %dynamic-slice_bitcast_fusion.2), channel_id=1, source_target_pairs={{0,8},{8,0},{16,24},{24,16},{1,9},{9,1},{17,25},{25,17},{2,10},{10... | collective-permute-start | bytes 3145736 | tf_op jit(solution)/shard_map/ppermute | solution.py:86
  274.5 14.8 %collective-permute-start.33 = (bf16[512,512]{1,0:T(8,128)(2,1)S(1)}, bf16[512,512]{1,0:T(8,128)(2,1)S(1)}, u32[]{:S(2)}, u32[]{:S(2)}) collective-permute-start(bf16[512,512]{1,0:T(8,128)(2,1)S(1)} %dynamic-slice_bitcast_fusion.3), channel_id=1, source_target_pairs={{0,16},{8,24},{16,0},{24,8},{1,17},{9,25},{17,1},{25,9},{2,18},{10... | collective-permute-start | bytes 1572872 | tf_op jit(solution)/shard_map/ppermute | solution.py:86
  277.6 17.6 %collective-permute-start.23 = (bf16[512,512]{1,0:T(8,128)(2,1)S(1)}, bf16[512,512]{1,0:T(8,128)(2,1)S(1)}, u32[]{:S(2)}, u32[]{:S(2)}) collective-permute-start(bf16[512,512]{1,0:T(8,128)(2,1)S(1)} %dynamic-slice_bitcast_fusion.4), channel_id=1, source_target_pairs={{0,1},{1,0},{2,3},{3,2},{4,5},{5,4},{6,7},{7,6},{8,9},{9,8},{10,11... | collective-permute-start | bytes 1572872 | tf_op jit(solution)/shard_map/ppermute | solution.py:86
  280.0 20.5 %collective-permute-start.3 = (bf16[512,512]{1,0:T(8,128)(2,1)S(1)}, bf16[512,512]{1,0:T(8,128)(2,1)S(1)}, u32[]{:S(2)}, u32[]{:S(2)}) collective-permute-start(bf16[512,512]{1,0:T(8,128)(2,1)S(1)} %dynamic-slice_bitcast_fusion.5), channel_id=1, source_target_pairs={{0,16},{8,24},{16,0},{24,8},{1,17},{9,25},{17,1},{25,9},{2,18},{10... | collective-permute-start | bytes 1572872 | tf_op jit(solution)/shard_map/ppermute | solution.py:86
  289.5 13.9 %collective-permute-start.34 = (bf16[256,512]{1,0:T(8,128)(2,1)S(1)}, bf16[256,512]{1,0:T(8,128)(2,1)S(1)}, u32[]{:S(2)}, u32[]{:S(2)}) collective-permute-start(bf16[256,512]{1,0:T(8,128)(2,1)S(1)} %dynamic-slice_bitcast_fusion.6), channel_id=1, source_target_pairs={{0,1},{1,0},{2,3},{3,2},{4,5},{5,4},{6,7},{7,6},{8,9},{9,8},{10,11... | collective-permute-start | bytes 786440 | tf_op jit(solution)/shard_map/ppermute | solution.py:86
  295.5 10.3 %collective-permute-start.24 = (bf16[256,512]{1,0:T(8,128)(2,1)S(1)}, bf16[256,512]{1,0:T(8,128)(2,1)S(1)}, u32[]{:S(2)}, u32[]{:S(2)}) collective-permute-start(bf16[256,512]{1,0:T(8,128)(2,1)S(1)} %dynamic-slice_bitcast_fusion.7), channel_id=1, source_target_pairs={{0,16},{8,24},{16,0},{24,8},{1,17},{9,25},{17,1},{25,9},{2,18},{10... | collective-permute-start | bytes 786440 | tf_op jit(solution)/shard_map/ppermute | solution.py:86
  301.5 16.6 %collective-permute-start.4 = (bf16[256,512]{1,0:T(8,128)(2,1)}, bf16[256,512]{1,0:T(8,128)(2,1)}, u32[]{:S(2)}, u32[]{:S(2)}) collective-permute-start(bf16[256,512]{1,0:T(8,128)(2,1)} %dynamic-slice_bitcast_fusion.9), channel_id=1, source_target_pairs={{0,1},{1,0},{2,3},{3,2},{4,5},{5,4},{6,7},{7,6},{8,9},{9,8},{10,11... | collective-permute-start | bytes 786440 | tf_op jit(solution)/shard_map/ppermute | solution.py:86
  304.3 17.1 %collective-permute-start.35 = (bf16[128,512]{1,0:T(8,128)(2,1)}, bf16[128,512]{1,0:T(8,128)(2,1)}, u32[]{:S(2)}, u32[]{:S(2)}) collective-permute-start(bf16[128,512]{1,0:T(8,128)(2,1)} %dynamic-slice_bitcast_fusion.10), channel_id=1, source_target_pairs={{0,2},{1,3},{2,0},{3,1},{4,6},{5,7},{6,4},{7,5},{8,10},{9,11},{10,... | collective-permute-start | bytes 393224 | tf_op jit(solution)/shard_map/ppermute | solution.py:86
  306.5 18.2 %collective-permute-start.25 = (bf16[128,512]{1,0:T(8,128)(2,1)}, bf16[128,512]{1,0:T(8,128)(2,1)}, u32[]{:S(2)}, u32[]{:S(2)}) collective-permute-start(bf16[128,512]{1,0:T(8,128)(2,1)} %dynamic-slice_bitcast_fusion.11), channel_id=1, source_target_pairs={{0,2},{1,3},{2,0},{3,1},{4,6},{5,7},{6,4},{7,5},{8,10},{9,11},{10,... | collective-permute-start | bytes 393224 | tf_op jit(solution)/shard_map/ppermute | solution.py:86
  313.6 36.2 %all-to-all-start.5 = ((bf16[8,2,128,128]{3,2,1,0:T(8,128)(2,1)}), bf16[8,2,128,128]{3,2,1,0:T(8,128)(2,1)S(1)}, u32[]{:S(2)}, u32[]{:S(2)}) async-start(bf16[8,2,128,128]{3,2,1,0:T(8,128)(2,1)} %broadcast_in_dim.118), calls=%async_computation.5 | async-start | bytes 1048576 | tf_op jit(solution)/shard_map/all_to_all | solution.py:109
  319.3 11.2 %collective-permute-start.5 = (bf16[128,512]{1,0:T(8,128)(2,1)S(1)}, bf16[128,512]{1,0:T(8,128)(2,1)S(1)}, u32[]{:S(2)}, u32[]{:S(2)}) collective-permute-start(bf16[128,512]{1,0:T(8,128)(2,1)S(1)} %dynamic-slice_bitcast_fusion.13), channel_id=1, source_target_pairs={{0,2},{1,3},{2,0},{3,1},{4,6},{5,7},{6,4},{7,5},{8,10},{9,11},{10,... | collective-permute-start | bytes 393224 | tf_op jit(solution)/shard_map/ppermute | solution.py:86
  322.3 17.9 %collective-permute-start.36 = (bf16[64,512]{1,0:T(8,128)(2,1)S(1)}, bf16[64,512]{1,0:T(8,128)(2,1)S(1)}, u32[]{:S(2)}, u32[]{:S(2)}) collective-permute-start(bf16[64,512]{1,0:T(8,128)(2,1)S(1)} %dynamic-slice_bitcast_fusion.14), channel_id=1, source_target_pairs={{0,4},{1,5},{2,6},{3,7},{4,0},{5,1},{6,2},{7,3},{8,12},{9,13},{10,... | collective-permute-start | bytes 196616 | tf_op jit(solution)/shard_map/ppermute | solution.py:86
  325.7 18.0 %collective-permute-start.26 = (bf16[64,512]{1,0:T(8,128)(2,1)S(1)}, bf16[64,512]{1,0:T(8,128)(2,1)S(1)}, u32[]{:S(2)}, u32[]{:S(2)}) collective-permute-start(bf16[64,512]{1,0:T(8,128)(2,1)S(1)} %dynamic-slice_bitcast_fusion.15), channel_id=1, source_target_pairs={{0,4},{1,5},{2,6},{3,7},{4,0},{5,1},{6,2},{7,3},{8,12},{9,13},{10,... | collective-permute-start | bytes 196616 | tf_op jit(solution)/shard_map/ppermute | solution.py:86
  330.5 15.5 %collective-permute-start.6 = (bf16[64,512]{1,0:T(8,128)(2,1)S(1)}, bf16[64,512]{1,0:T(8,128)(2,1)S(1)}, u32[]{:S(2)}, u32[]{:S(2)}) collective-permute-start(bf16[64,512]{1,0:T(8,128)(2,1)S(1)} %dynamic-slice_bitcast_fusion.17), channel_id=1, source_target_pairs={{0,4},{1,5},{2,6},{3,7},{4,0},{5,1},{6,2},{7,3},{8,12},{9,13},{10,... | collective-permute-start | bytes 196616 | tf_op jit(solution)/shard_map/ppermute | solution.py:86
  340.2 7.4 %collective-permute-start.37 = (bf16[64,512]{1,0:T(8,128)(2,1)S(1)}, bf16[64,512]{1,0:T(8,128)(2,1)S(1)}, u32[]{:S(2)}, u32[]{:S(2)}) collective-permute-start(bf16[64,512]{1,0:T(8,128)(2,1)S(1)} %fusion.93), channel_id=1, source_target_pairs={{0,4},{1,5},{2,6},{3,7},{4,0},{5,1},{6,2},{7,3},{8,12},{9,13},{10,... | collective-permute-start | bytes 196616 | tf_op jit(solution)/shard_map/ppermute | solution.py:86
  343.7 5.3 %collective-permute-start.27 = (bf16[64,512]{1,0:T(8,128)(2,1)S(1)}, bf16[64,512]{1,0:T(8,128)(2,1)S(1)}, u32[]{:S(2)}, u32[]{:S(2)}) collective-permute-start(bf16[64,512]{1,0:T(8,128)(2,1)S(1)} %fusion.94), channel_id=1, source_target_pairs={{0,4},{1,5},{2,6},{3,7},{4,0},{5,1},{6,2},{7,3},{8,12},{9,13},{10,... | collective-permute-start | bytes 196616 | tf_op jit(solution)/shard_map/ppermute | solution.py:86
  346.0 15.7 %collective-permute-start.7 = (bf16[64,512]{1,0:T(8,128)(2,1)S(1)}, bf16[64,512]{1,0:T(8,128)(2,1)S(1)}, u32[]{:S(2)}, u32[]{:S(2)}) collective-permute-start(bf16[64,512]{1,0:T(8,128)(2,1)S(1)} %fusion.96), channel_id=1, source_target_pairs={{0,4},{1,5},{2,6},{3,7},{4,0},{5,1},{6,2},{7,3},{8,12},{9,13},{10,... | collective-permute-start | bytes 196616 | tf_op jit(solution)/shard_map/ppermute | solution.py:86
  347.6 16.2 %collective-permute-start.38 = (bf16[128,512]{1,0:T(8,128)(2,1)S(1)}, bf16[128,512]{1,0:T(8,128)(2,1)S(1)}, u32[]{:S(2)}, u32[]{:S(2)}) collective-permute-start(bf16[128,512]{1,0:T(8,128)(2,1)S(1)} %bitcast.485), channel_id=1, source_target_pairs={{0,2},{1,3},{2,0},{3,1},{4,6},{5,7},{6,4},{7,5},{8,10},{9,11},{10,... | collective-permute-start | bytes 393224 | tf_op jit(solution)/shard_map/ppermute | solution.py:86
  349.1 16.3 %collective-permute-start.28 = (bf16[128,512]{1,0:T(8,128)(2,1)S(1)}, bf16[128,512]{1,0:T(8,128)(2,1)S(1)}, u32[]{:S(2)}, u32[]{:S(2)}) collective-permute-start(bf16[128,512]{1,0:T(8,128)(2,1)S(1)} %bitcast.487), channel_id=1, source_target_pairs={{0,2},{1,3},{2,0},{3,1},{4,6},{5,7},{6,4},{7,5},{8,10},{9,11},{10,... | collective-permute-start | bytes 393224 | tf_op jit(solution)/shard_map/ppermute | solution.py:86
  349.8 66.7 %all-to-all-start.4 = ((bf16[8,2,4,16,512]{4,2,3,1,0:T(4,128)(2,1)}), bf16[8,2,4,16,512]{4,2,3,1,0:T(4,128)(2,1)}, u32[]{:S(2)}, u32[]{:S(2)}) async-start(bf16[8,2,4,16,512]{4,2,3,1,0:T(4,128)(2,1)} %bitcast.418), calls=%async_computation.4 | async-start | bytes 2097152 | tf_op jit(solution)/shard_map/all_to_all | solution.py:302
  361.7 5.3 %collective-permute-start.12 = (bf16[256,512]{1,0:T(8,128)(2,1)S(1)}, bf16[256,512]{1,0:T(8,128)(2,1)S(1)}, u32[]{:S(2)}, u32[]{:S(2)}) collective-permute-start(bf16[256,512]{1,0:T(8,128)(2,1)S(1)} %dynamic-slice_bitcast_fusion.8), channel_id=1, source_target_pairs={{0,8},{8,0},{16,24},{24,16},{1,9},{9,1},{17,25},{25,17},{2,10},{10... | collective-permute-start | bytes 786440 | tf_op jit(solution)/shard_map/ppermute | solution.py:86
  361.8 9.7 %collective-permute-start.8 = (bf16[128,512]{1,0:T(8,128)(2,1)S(1)}, bf16[128,512]{1,0:T(8,128)(2,1)S(1)}, u32[]{:S(2)}, u32[]{:S(2)}) collective-permute-start(bf16[128,512]{1,0:T(8,128)(2,1)S(1)} %bitcast.489), channel_id=1, source_target_pairs={{0,2},{1,3},{2,0},{3,1},{4,6},{5,7},{6,4},{7,5},{8,10},{9,11},{10,... | collective-permute-start | bytes 393224 | tf_op jit(solution)/shard_map/ppermute | solution.py:86
  363.9 10.9 %collective-permute-start.39 = (bf16[256,512]{1,0:T(8,128)(2,1)S(1)}, bf16[256,512]{1,0:T(8,128)(2,1)S(1)}, u32[]{:S(2)}, u32[]{:S(2)}) collective-permute-start(bf16[256,512]{1,0:T(8,128)(2,1)S(1)} %bitcast.471), channel_id=1, source_target_pairs={{0,1},{1,0},{2,3},{3,2},{4,5},{5,4},{6,7},{7,6},{8,9},{9,8},{10,11... | collective-permute-start | bytes 786440 | tf_op jit(solution)/shard_map/ppermute | solution.py:86
  365.4 13.8 %collective-permute-start.29 = (bf16[256,512]{1,0:T(8,128)(2,1)S(1)}, bf16[256,512]{1,0:T(8,128)(2,1)S(1)}, u32[]{:S(2)}, u32[]{:S(2)}) collective-permute-start(bf16[256,512]{1,0:T(8,128)(2,1)S(1)} %bitcast.467), channel_id=1, source_target_pairs={{0,16},{8,24},{16,0},{24,8},{1,17},{9,25},{17,1},{25,9},{2,18},{10... | collective-permute-start | bytes 786440 | tf_op jit(solution)/shard_map/ppermute | solution.py:86
  367.1 10.5 %collective-permute-start.13 = (bf16[128,512]{1,0:T(8,128)(2,1)S(1)}, bf16[128,512]{1,0:T(8,128)(2,1)S(1)}, u32[]{:S(2)}, u32[]{:S(2)}) collective-permute-start(bf16[128,512]{1,0:T(8,128)(2,1)S(1)} %dynamic-slice_bitcast_fusion.12), channel_id=1, source_target_pairs={{0,1},{1,0},{2,3},{3,2},{4,5},{5,4},{6,7},{7,6},{8,9},{9,8},{10,11... | collective-permute-start | bytes 393224 | tf_op jit(solution)/shard_map/ppermute | solution.py:86
  371.6 18.1 %collective-permute-start.9 = (bf16[256,512]{1,0:T(8,128)(2,1)S(1)}, bf16[256,512]{1,0:T(8,128)(2,1)S(1)}, u32[]{:S(2)}, u32[]{:S(2)}) collective-permute-start(bf16[256,512]{1,0:T(8,128)(2,1)S(1)} %bitcast.469), channel_id=1, source_target_pairs={{0,1},{1,0},{2,3},{3,2},{4,5},{5,4},{6,7},{7,6},{8,9},{9,8},{10,11... | collective-permute-start | bytes 786440 | tf_op jit(solution)/shard_map/ppermute | solution.py:86
  374.9 28.3 %collective-permute-start.40 = (bf16[512,512]{1,0:T(8,128)(2,1)S(1)}, bf16[512,512]{1,0:T(8,128)(2,1)S(1)}, u32[]{:S(2)}, u32[]{:S(2)}) collective-permute-start(bf16[512,512]{1,0:T(8,128)(2,1)S(1)} %bitcast.451), channel_id=1, source_target_pairs={{0,16},{8,24},{16,0},{24,8},{1,17},{9,25},{17,1},{25,9},{2,18},{10... | collective-permute-start | bytes 1572872 | tf_op jit(solution)/shard_map/ppermute | solution.py:86
  377.7 11.8 %collective-permute-start.14 = (bf16[64,512]{1,0:T(8,128)(2,1)S(1)}, bf16[64,512]{1,0:T(8,128)(2,1)S(1)}, u32[]{:S(2)}, u32[]{:S(2)}) collective-permute-start(bf16[64,512]{1,0:T(8,128)(2,1)S(1)} %dynamic-slice_bitcast_fusion.16), channel_id=1, source_target_pairs={{0,16},{8,24},{16,0},{24,8},{1,17},{9,25},{17,1},{25,9},{2,18},{10... | collective-permute-start | bytes 196616 | tf_op jit(solution)/shard_map/ppermute | solution.py:86
  379.3 29.3 %collective-permute-start.30 = (bf16[512,512]{1,0:T(8,128)(2,1)S(1)}, bf16[512,512]{1,0:T(8,128)(2,1)S(1)}, u32[]{:S(2)}, u32[]{:S(2)}) collective-permute-start(bf16[512,512]{1,0:T(8,128)(2,1)S(1)} %bitcast.453), channel_id=1, source_target_pairs={{0,1},{1,0},{2,3},{3,2},{4,5},{5,4},{6,7},{7,6},{8,9},{9,8},{10,11... | collective-permute-start | bytes 1572872 | tf_op jit(solution)/shard_map/ppermute | solution.py:86
  389.5 4.0 collective-permute-start.15
  389.7 22.0 %collective-permute-start.10 = (bf16[512,512]{1,0:T(8,128)(2,1)S(1)}, bf16[512,512]{1,0:T(8,128)(2,1)S(1)}, u32[]{:S(2)}, u32[]{:S(2)}) collective-permute-start(bf16[512,512]{1,0:T(8,128)(2,1)S(1)} %bitcast.455), channel_id=1, source_target_pairs={{0,16},{8,24},{16,0},{24,8},{1,17},{9,25},{17,1},{25,9},{2,18},{10... | collective-permute-start | bytes 1572872 | tf_op jit(solution)/shard_map/ppermute | solution.py:86
  393.6 4.8 %collective-permute-start.16 = (bf16[16,512]{1,0:T(8,128)(2,1)S(1)}, bf16[16,512]{1,0:T(8,128)(2,1)S(1)}, u32[]{:S(2)}, u32[]{:S(2)}) collective-permute-start(bf16[16,512]{1,0:T(8,128)(2,1)S(1)} %dynamic-slice_bitcast_fusion.19), channel_id=1, source_target_pairs={{0,4},{1,5},{2,6},{3,7},{4,0},{5,1},{6,2},{7,3},{8,12},{9,13},{10,... | collective-permute-start | bytes 49160 | tf_op jit(solution)/shard_map/ppermute | solution.py:86
  398.4 4.7 %collective-permute-start.17 = (bf16[16,512]{1,0:T(8,128)(2,1)S(1)}, bf16[16,512]{1,0:T(8,128)(2,1)S(1)}, u32[]{:S(2)}, u32[]{:S(2)}) collective-permute-start(bf16[16,512]{1,0:T(8,128)(2,1)S(1)} %fusion.124), channel_id=1, source_target_pairs={{0,4},{1,5},{2,6},{3,7},{4,0},{5,1},{6,2},{7,3},{8,12},{9,13},{10,... | collective-permute-start | bytes 49160 | tf_op jit(solution)/shard_map/ppermute | solution.py:86
  403.1 4.0 collective-permute-start.18
  404.3 45.2 %collective-permute-start.41 = (bf16[1024,512]{1,0:T(8,128)(2,1)}, bf16[1024,512]{1,0:T(8,128)(2,1)}, u32[]{:S(2)}, u32[]{:S(2)}) collective-permute-start(bf16[1024,512]{1,0:T(8,128)(2,1)} %bitcast.178), channel_id=1, source_target_pairs={{0,8},{8,0},{16,24},{24,16},{1,9},{9,1},{17,25},{25,17},{2,10},{10... | collective-permute-start | bytes 3145736 | tf_op jit(solution)/shard_map/ppermute | solution.py:86
  407.1 4.3 collective-permute-start.19
  409.8 31.0 %collective-permute-start.31 = (bf16[1024,512]{1,0:T(8,128)(2,1)}, bf16[1024,512]{1,0:T(8,128)(2,1)}, u32[]{:S(2)}, u32[]{:S(2)}) collective-permute-start(bf16[1024,512]{1,0:T(8,128)(2,1)} %bitcast.147), channel_id=1, source_target_pairs={{0,8},{8,0},{16,24},{24,16},{1,9},{9,1},{17,25},{25,17},{2,10},{10... | collective-permute-start | bytes 3145736 | tf_op jit(solution)/shard_map/ppermute | solution.py:86
  411.4 5.0 %collective-permute-start.20 = (bf16[128,512]{1,0:T(8,128)(2,1)S(1)}, bf16[128,512]{1,0:T(8,128)(2,1)S(1)}, u32[]{:S(2)}, u32[]{:S(2)}) collective-permute-start(bf16[128,512]{1,0:T(8,128)(2,1)S(1)} %bitcast.491), channel_id=1, source_target_pairs={{0,1},{1,0},{2,3},{3,2},{4,5},{5,4},{6,7},{7,6},{8,9},{9,8},{10,11... | collective-permute-start | bytes 393224 | tf_op jit(solution)/shard_map/ppermute | solution.py:86
  412.8 30.7 %collective-permute-start.11 = (bf16[1024,512]{1,0:T(8,128)(2,1)}, bf16[1024,512]{1,0:T(8,128)(2,1)}, u32[]{:S(2)}, u32[]{:S(2)}) collective-permute-start(bf16[1024,512]{1,0:T(8,128)(2,1)} %bitcast.80), channel_id=1, source_target_pairs={{0,8},{8,0},{16,24},{24,16},{1,9},{9,1},{17,25},{25,17},{2,10},{10... | collective-permute-start | bytes 3145736 | tf_op jit(solution)/shard_map/ppermute | solution.py:86
  416.5 22.0 %collective-permute-start.21 = (bf16[256,512]{1,0:T(8,128)(2,1)S(1)}, bf16[256,512]{1,0:T(8,128)(2,1)}, u32[]{:S(2)}, u32[]{:S(2)}) collective-permute-start(bf16[256,512]{1,0:T(8,128)(2,1)S(1)} %bitcast.465), channel_id=1, source_target_pairs={{0,8},{8,0},{16,24},{24,16},{1,9},{9,1},{17,25},{25,17},{2,10},{10... | collective-permute-start | bytes 786440 | tf_op jit(solution)/shard_map/ppermute | solution.py:86
  430.5 26.4 %all-to-all-start.6 = ((f32[32,8,512]{2,1,0:T(8,128)}), f32[32,8,512]{2,1,0:T(8,128)}, u32[]{:S(2)}, u32[]{:S(2)}) async-start(f32[32,8,512]{2,1,0:T(8,128)} %broadcast_in_dim.220), calls=%async_computation.6 | async-start | bytes 1048576 | tf_op jit(solution)/shard_map/all_to_all | solution.py:349
  (130 other events, 741.8 us)
